TPU v7x, 32 devices: a whole 2x2x4 slice. The times are simulated.
32 devices in a mesh: dp: 2 (over x), context: 8 (over z, y), tensor: 2 (over core).
Axes of the slice: x: 2, y: 2, z: 4, core: 2. Of those that a mesh axis runs over, the one named last changes fastest.
Arguments:
- tokens: bfloat16 [4096, 2, 1536], P('context', 'dp'), may hold values from -6 to 6
- positions: int32 [4096, 2], P('context', 'dp'), may hold values from 0 to 4095, as said below
- gain_one: bfloat16 [1536], P(('dp', 'context')), may hold values from 0.099609375 to 1.8984375
- gain_two: bfloat16 [1536], P(('dp', 'context')), may hold values from 0.099609375 to 1.8984375
- w_query: bfloat16 [1536, 1536], P(('dp', 'context'), 'tensor'), may hold values from -0.15625 to 0.15625
- w_key: bfloat16 [1536, 768], P(('dp', 'context'), 'tensor'), may hold values from -0.15625 to 0.15625
- w_value: bfloat16 [1536, 768], P(('dp', 'context'), 'tensor'), may hold values from -0.15625 to 0.15625
- w_out: bfloat16 [1536, 1536], P('tensor', ('dp', 'context')), may hold values from -0.875 to 0.875
- w_gate: bfloat16 [1536, 4096], P(('dp', 'context'), 'tensor'), may hold values from -0.15625 to 0.15625
- w_up: bfloat16 [1536, 4096], P(('dp', 'context'), 'tensor'), may hold values from -0.15625 to 0.15625
- w_down: bfloat16 [4096, 1536], P('tensor', ('dp', 'context')), may hold values from -0.09375 to 0.09375
- cotangent: bfloat16 [4096, 2, 1536], P('context', 'dp'), may hold values from -6 to 6
Outputs:
- layer_out: bfloat16 [4096, 2, 1536], P('context', 'dp')
- input_grad: float32 [4096, 2, 1536], P('context', 'dp')
- grad_gain_one: float32 [1536], P(('dp', 'context'))
- grad_gain_two: float32 [1536], P(('dp', 'context'))
- grad_query: float32 [1536, 1536], P(('dp', 'context'), 'tensor')
- grad_key: float32 [1536, 768], P(('dp', 'context'), 'tensor')
- grad_value: float32 [1536, 768], P(('dp', 'context'), 'tensor')
- grad_out: float32 [1536, 1536], P('tensor', ('dp', 'context'))
- grad_gate: float32 [1536, 4096], P(('dp', 'context'), 'tensor')
- grad_up: float32 [1536, 4096], P(('dp', 'context'), 'tensor')
- grad_down: float32 [4096, 1536], P('tensor', ('dp', 'context'))
Inputs may be any that keep to these rules, and one draw needn't show every extreme that they name: In every sequence the positions are each of 0 to 4095 once; the 512 slots of one index of context hold two runs of 256 consecutive positions, block c in the first half and block 15 - c in the second, with c different for each index of context.
All inputs are finite; a program needn't handle non-finite values.
Results may differ from a plain program's by a relative error of at most 0.02.
Values may be sent and summed in bfloat16 or wider, within the bound.
A program may use at most 256 MiB of HBM per device.

v0:
```python
import functools

import jax
import jax.numpy as jnp
import numpy as np
from jax import lax
from jax.experimental import pallas as pl
from jax.experimental.pallas import tpu as pltpu
from jax.sharding import PartitionSpec as P

HEAD = 96


epsilon = 1e-05
theta_base = 100000.0
masked_value = -1e30


def norm_forward(values_in, gain_vec):
    inverse = lax.rsqrt(jnp.mean(values_in * values_in, axis=-1, keepdims=True) + epsilon)
    unit_vals = values_in * inverse
    return (unit_vals, inverse, (unit_vals * gain_vec.astype(jnp.float32)).astype(jnp.bfloat16))


def norm_backward(grad_in, unit_vals, inverse, gain_vec):
    scaled = grad_in * gain_vec.astype(jnp.float32)
    grad_vals = inverse * (
        scaled - unit_vals * jnp.mean(scaled * unit_vals, axis=-1, keepdims=True)
    )
    return (grad_vals, jnp.sum(grad_in * unit_vals, axis=0))


def rotate(values_in, cos_part, sin_part):
    half_size = values_in.shape[-1] // 2
    front_half = values_in[..., :half_size]
    back_half = values_in[..., half_size:]
    return jnp.concatenate(
        [
            front_half * cos_part - back_half * sin_part,
            back_half * cos_part + front_half * sin_part,
        ],
        axis=-1,
    )


def contract_rows(left_mat, right_mat):
    return lax.dot_general(
        left_mat, right_mat, (((0,), (0,)), ((), ())), preferred_element_type=jnp.float32
    )


def contract_cols(left_mat, right_mat):
    return lax.dot_general(
        left_mat, right_mat, (((1,), (1,)), ((), ())), preferred_element_type=jnp.float32
    )


def on_device(
    tokens,
    positions,
    gain_one,
    gain_two,
    w_query,
    w_key,
    w_value,
    w_out,
    w_gate,
    w_up,
    w_down,
    cotangent,
):
    slot_count, seq_count, model_width = tokens.shape
    row_count = slot_count * seq_count
    gathered = (
        lax.all_gather(gain_one, ("dp", "context"), axis=0, tiled=True),
        lax.all_gather(gain_two, ("dp", "context"), axis=0, tiled=True),
        lax.all_gather(w_query, ("dp", "context"), axis=0, tiled=True),
        lax.all_gather(w_key, ("dp", "context"), axis=0, tiled=True),
        lax.all_gather(w_value, ("dp", "context"), axis=0, tiled=True),
        lax.all_gather(w_out, ("dp", "context"), axis=1, tiled=True),
        lax.all_gather(w_gate, ("dp", "context"), axis=0, tiled=True),
        lax.all_gather(w_up, ("dp", "context"), axis=0, tiled=True),
        lax.all_gather(w_down, ("dp", "context"), axis=1, tiled=True),
    )
    full_one, full_two, query_mat, key_mat, value_mat, out_mat, gate_mat, up_mat, down_mat = (
        gathered
    )
    heads_kv = key_mat.shape[1] // HEAD
    heads_q = query_mat.shape[1] // HEAD
    group_size = heads_q // heads_kv
    score_scale = HEAD ** (-0.5)
    half_size = HEAD // 2
    inv_freqs = theta_base ** (-2.0 * jnp.arange(half_size, dtype=jnp.float32) / HEAD)
    angles = positions.astype(jnp.float32)[:, :, None] * inv_freqs
    cos_part = jnp.cos(angles)[:, :, None, :]
    sin_part = jnp.sin(angles)[:, :, None, :]
    flat_in = tokens.astype(jnp.float32).reshape(row_count, model_width)
    unit_one, inverse_one, normed = norm_forward(flat_in, full_one)
    query_proj = jnp.dot(normed, query_mat, preferred_element_type=jnp.float32).reshape(
        slot_count, seq_count, heads_q, HEAD
    )
    key_proj = jnp.dot(normed, key_mat, preferred_element_type=jnp.float32).reshape(
        slot_count, seq_count, heads_kv, HEAD
    )
    value_low = (
        jnp.dot(normed, value_mat, preferred_element_type=jnp.float32)
        .astype(jnp.bfloat16)
        .reshape(slot_count, seq_count, heads_kv * HEAD)
    )
    queries = rotate(query_proj, cos_part, sin_part).astype(jnp.bfloat16)
    keys_low = (
        rotate(key_proj, cos_part, sin_part)
        .astype(jnp.bfloat16)
        .reshape(slot_count, seq_count, heads_kv * HEAD)
    )
    query_seq = jnp.transpose(
        queries.reshape(slot_count, seq_count, heads_kv, group_size, HEAD), (1, 2, 3, 0, 4)
    )
    query_pos = positions.T
    stat_shape = (seq_count, heads_kv, group_size, slot_count)
    initial = (
        jnp.full(stat_shape, masked_value, jnp.float32),
        jnp.zeros(stat_shape, jnp.float32),
        jnp.zeros(stat_shape + (HEAD,), jnp.float32),
    )
    key_piece = lax.all_gather(keys_low, "context", axis=0, tiled=True)
    value_piece = lax.all_gather(value_low, "context", axis=0, tiled=True)
    pos_piece = lax.all_gather(positions, "context", axis=0, tiled=True)
    piece_len = key_piece.shape[0]
    key_seq = jnp.transpose(key_piece.reshape(piece_len, seq_count, heads_kv, HEAD), (1, 2, 0, 3))
    value_seq = jnp.transpose(
        value_piece.reshape(piece_len, seq_count, heads_kv, HEAD), (1, 2, 0, 3)
    )
    pos_seq = pos_piece.T

    def per_sequence(seq_items):
        peak_val, totals, accum_vals, query_one, qpos_one, key_one, value_one, kpos_one = seq_items
        raw_scores = (
            jnp.einsum("hgqd,hkd->hgqk", query_one, key_one, preferred_element_type=jnp.float32)
            * score_scale
        )
        allowed = kpos_one[None, None, None, :] <= qpos_one[None, None, :, None]
        masked = jnp.where(allowed, raw_scores, masked_value)
        new_peak = jnp.maximum(peak_val, jnp.max(masked, axis=-1))
        decay_vals = jnp.exp(peak_val - new_peak)
        weights = jnp.where(allowed, jnp.exp(masked - new_peak[..., None]), 0.0)
        totals = totals * decay_vals + jnp.sum(weights, axis=-1)
        accum_vals = accum_vals * decay_vals[..., None] + jnp.einsum(
            "hgqk,hkd->hgqd",
            weights.astype(jnp.bfloat16),
            value_one,
            preferred_element_type=jnp.float32,
        )
        return (new_peak, totals, accum_vals)

    peak_val, totals, accum_vals = lax.map(
        per_sequence,
        (initial[0], initial[1], initial[2], query_seq, query_pos, key_seq, value_seq, pos_seq),
    )
    log_total = peak_val + jnp.log(totals)
    mixed_seq = accum_vals / totals[..., None]
    mixed_low = (
        jnp.transpose(mixed_seq, (3, 0, 1, 2, 4))
        .reshape(row_count, heads_q * HEAD)
        .astype(jnp.bfloat16)
    )
    branch = lax.psum(
        jnp.dot(mixed_low, out_mat, preferred_element_type=jnp.float32).astype(jnp.bfloat16),
        "tensor",
    ).astype(jnp.float32)
    middle = flat_in + branch
    unit_two, inverse_two, second = norm_forward(middle, full_two)
    gate_vals = jnp.dot(second, gate_mat, preferred_element_type=jnp.float32)
    up_vals = jnp.dot(second, up_mat, preferred_element_type=jnp.float32)
    sigmoid_vals = jax.nn.sigmoid(gate_vals)
    silu_vals = gate_vals * sigmoid_vals
    hidden = (silu_vals * up_vals).astype(jnp.bfloat16)
    mlp_part = lax.psum(
        jnp.dot(hidden, down_mat, preferred_element_type=jnp.float32).astype(jnp.bfloat16), "tensor"
    ).astype(jnp.float32)
    layer_out = (middle + mlp_part).astype(jnp.bfloat16).reshape(slot_count, seq_count, model_width)
    regathered = (
        lax.all_gather(gain_one, ("dp", "context"), axis=0, tiled=True),
        lax.all_gather(gain_two, ("dp", "context"), axis=0, tiled=True),
        lax.all_gather(w_query, ("dp", "context"), axis=0, tiled=True),
        lax.all_gather(w_key, ("dp", "context"), axis=0, tiled=True),
        lax.all_gather(w_value, ("dp", "context"), axis=0, tiled=True),
        lax.all_gather(w_out, ("dp", "context"), axis=1, tiled=True),
        lax.all_gather(w_gate, ("dp", "context"), axis=0, tiled=True),
        lax.all_gather(w_up, ("dp", "context"), axis=0, tiled=True),
        lax.all_gather(w_down, ("dp", "context"), axis=1, tiled=True),
    )
    full_one, full_two, query_mat, key_mat, value_mat, out_mat, gate_mat, up_mat, down_mat = (
        regathered
    )
    grad_low = cotangent.reshape(row_count, model_width)
    grad_down = contract_rows(hidden, grad_low)
    grad_hidden = contract_cols(grad_low, down_mat)
    grad_gate_low = (
        grad_hidden * up_vals * sigmoid_vals * (1.0 + gate_vals * (1.0 - sigmoid_vals))
    ).astype(jnp.bfloat16)
    grad_up_low = (grad_hidden * silu_vals).astype(jnp.bfloat16)
    grad_gate = contract_rows(second, grad_gate_low)
    grad_up = contract_rows(second, grad_up_low)
    grad_second = lax.psum(
        (contract_cols(grad_gate_low, gate_mat) + contract_cols(grad_up_low, up_mat)).astype(
            jnp.bfloat16
        ),
        "tensor",
    ).astype(jnp.float32)
    grad_mid_norm, grad_gain_two = norm_backward(grad_second, unit_two, inverse_two, full_two)
    grad_middle = grad_low.astype(jnp.float32) + grad_mid_norm
    grad_mid_low = grad_middle.astype(jnp.bfloat16)
    grad_out = contract_rows(mixed_low, grad_mid_low)
    grad_mixed = contract_cols(grad_mid_low, out_mat).astype(jnp.bfloat16)
    grad_mixed_seq = jnp.transpose(
        grad_mixed.reshape(slot_count, seq_count, heads_kv, group_size, HEAD), (1, 2, 3, 0, 4)
    )
    delta_rows = jnp.sum(grad_mixed_seq.astype(jnp.float32) * mixed_seq, axis=-1)
    kv_width = heads_kv * HEAD

    def block_grads(grad_query_acc, key_blk, value_blk, pos_blk):
        block_len = key_blk.shape[0]
        key_seq = jnp.transpose(key_blk.reshape(block_len, seq_count, heads_kv, HEAD), (1, 2, 0, 3))
        value_seq = jnp.transpose(
            value_blk.reshape(block_len, seq_count, heads_kv, HEAD), (1, 2, 0, 3)
        )
        raw_scores = (
            jnp.einsum("shgqd,shkd->shgqk", query_seq, key_seq, preferred_element_type=jnp.float32)
            * score_scale
        )
        allowed = pos_blk.T[:, None, None, None, :] <= query_pos[:, None, None, :, None]
        prob_vals = jnp.where(
            allowed,
            jnp.exp(jnp.where(allowed, raw_scores - log_total[..., None], masked_value)),
            0.0,
        )
        grad_value_blk = jnp.einsum(
            "shgqk,shgqd->kshd",
            prob_vals.astype(jnp.bfloat16),
            grad_mixed_seq,
            preferred_element_type=jnp.float32,
        )
        grad_probs = jnp.einsum(
            "shgqd,shkd->shgqk", grad_mixed_seq, value_seq, preferred_element_type=jnp.float32
        )
        grad_scores = (prob_vals * (grad_probs - delta_rows[..., None])).astype(jnp.bfloat16)
        grad_query_acc = grad_query_acc + jnp.einsum(
            "shgqk,shkd->shgqd", grad_scores, key_seq, preferred_element_type=jnp.float32
        )
        grad_key_blk = jnp.einsum(
            "shgqk,shgqd->kshd", grad_scores, query_seq, preferred_element_type=jnp.float32
        )
        return (
            grad_query_acc,
            grad_key_blk.reshape(block_len, seq_count, kv_width),
            grad_value_blk.reshape(block_len, seq_count, kv_width),
        )

    zero_query = jnp.zeros(stat_shape + (HEAD,), jnp.float32)
    key_all, value_all, pos_all = (
        lax.all_gather(keys_low, "context", axis=0, tiled=True),
        lax.all_gather(value_low, "context", axis=0, tiled=True),
        lax.all_gather(positions, "context", axis=0, tiled=True),
    )
    total_len = key_all.shape[0]
    block_size = min(512, total_len)
    block_count = total_len // block_size

    def key_block(grad_query_acc, block_items):
        key_blk, value_blk, pos_blk = block_items
        grad_query_acc, grad_key_blk, grad_value_blk = block_grads(
            grad_query_acc, key_blk, value_blk, pos_blk
        )
        return (grad_query_acc, (grad_key_blk, grad_value_blk))

    grad_query_acc, (grad_keys_all, grad_values_all) = lax.scan(
        key_block,
        zero_query,
        (
            key_all.reshape(block_count, block_size, seq_count, kv_width),
            value_all.reshape(block_count, block_size, seq_count, kv_width),
            pos_all.reshape(block_count, block_size, seq_count),
        ),
    )
    grad_key_own, grad_value_own = (
        lax.psum_scatter(
            grad_keys_all.reshape(total_len, seq_count, kv_width).astype(jnp.bfloat16),
            "context",
            scatter_dimension=0,
            tiled=True,
        ).astype(jnp.float32),
        lax.psum_scatter(
            grad_values_all.reshape(total_len, seq_count, kv_width).astype(jnp.bfloat16),
            "context",
            scatter_dimension=0,
            tiled=True,
        ).astype(jnp.float32),
    )
    grad_rot_q = jnp.transpose(grad_query_acc * score_scale, (3, 0, 1, 2, 4)).reshape(
        slot_count, seq_count, heads_q, HEAD
    )
    grad_q_low = (
        rotate(grad_rot_q, cos_part, -sin_part)
        .reshape(row_count, heads_q * HEAD)
        .astype(jnp.bfloat16)
    )
    grad_rot_k = (grad_key_own * score_scale).reshape(slot_count, seq_count, heads_kv, HEAD)
    grad_k_low = (
        rotate(grad_rot_k, cos_part, -sin_part).reshape(row_count, kv_width).astype(jnp.bfloat16)
    )
    grad_v_low = grad_value_own.reshape(row_count, kv_width).astype(jnp.bfloat16)
    grad_query = contract_rows(normed, grad_q_low)
    grad_key = contract_rows(normed, grad_k_low)
    grad_value = contract_rows(normed, grad_v_low)
    grad_normed = lax.psum(
        (
            contract_cols(grad_q_low, query_mat)
            + contract_cols(grad_k_low, key_mat)
            + contract_cols(grad_v_low, value_mat)
        ).astype(jnp.bfloat16),
        "tensor",
    ).astype(jnp.float32)
    grad_in_norm, grad_gain_one = norm_backward(grad_normed, unit_one, inverse_one, full_one)
    input_grad = (grad_middle + grad_in_norm).reshape(slot_count, seq_count, model_width)
    reduced = (
        lax.psum_scatter(grad_gain_one, ("dp", "context"), scatter_dimension=0, tiled=True),
        lax.psum_scatter(grad_gain_two, ("dp", "context"), scatter_dimension=0, tiled=True),
        lax.psum_scatter(grad_query, ("dp", "context"), scatter_dimension=0, tiled=True),
        lax.psum_scatter(grad_key, ("dp", "context"), scatter_dimension=0, tiled=True),
        lax.psum_scatter(grad_value, ("dp", "context"), scatter_dimension=0, tiled=True),
        lax.psum_scatter(grad_out, ("dp", "context"), scatter_dimension=1, tiled=True),
        lax.psum_scatter(grad_gate, ("dp", "context"), scatter_dimension=0, tiled=True),
        lax.psum_scatter(grad_up, ("dp", "context"), scatter_dimension=0, tiled=True),
        lax.psum_scatter(grad_down, ("dp", "context"), scatter_dimension=1, tiled=True),
    )
    return (
        layer_out,
        input_grad,
        reduced[0],
        reduced[1],
        reduced[2],
        reduced[3],
        reduced[4],
        reduced[5],
        reduced[6],
        reduced[7],
        reduced[8],
    )


WIDE = 128
HALF = HEAD // 2
RUN = 256
TILE = 512
LOG2_E = 1.4426950408889634
MESH = pl.DeviceIdType.MESH
PIECE = 256
FEED = 512
VMEM_LIMIT = 56 * 1024 * 1024


def any_spec():
    return pl.BlockSpec(memory_space=pl.ANY)


def vmem_spec():
    return pl.BlockSpec(memory_space=pltpu.VMEM)


def place():
    return lax.axis_index("dp"), lax.axis_index("context"), lax.axis_index("tensor")


def greet(devices):
    barrier = pltpu.get_barrier_semaphore()
    for device in devices:
        pl.semaphore_signal(barrier, inc=1, device_id=device, device_id_type=MESH)
    pl.semaphore_wait(barrier, len(devices))


def sequence_others():
    row, spot, core = place()
    return [
        (row, lax.rem(spot + shift, 8), lax.rem(core + flip, 2))
        for shift in range(8)
        for flip in range(2)
        if shift or flip
    ]


def lane_freqs():
    return jnp.asarray(
        np.power(np.float32(theta_base), np.float32(-2.0) * np.arange(HALF, dtype=np.float32) / HEAD)
    ).reshape(HALF, 1)


def dot_f32(left, right):
    return jnp.dot(left, right, preferred_element_type=jnp.float32)


def own_shard():
    row, spot, core = place()
    return row * 8 + spot


def group_others():
    row, spot, core = place()
    return sequence_others() + [(1 - row, lax.rem(spot + shift, 8), core) for shift in range(8)]


def exchange_messages(message_to, landing, send, recv):
    row, spot, core = place()
    copies, waits = [], []

    def one(flip, shift):
        at = flip * 8 + shift
        to_row = lax.rem(row + flip, 2)
        chip, source = lax.rem(spot + shift, 8), lax.rem(spot + 8 - shift, 8)
        device = (to_row, chip, core)
        message = message_to(to_row * 8 + chip)
        copies.append(
            remote(message, landing.at[row * 8 + spot], send.at[at], recv.at[at], device)
        )
        came = landing.at[to_row * 8 + source]
        waits.append(remote(came, came, send.at[at], recv.at[at], device).wait_recv)

    for flip in range(2):
        for shift in range(8):
            if flip or shift:
                one(flip, shift)
    return copies, waits


def turn_left(left_t, index, source):
    quarter = source.shape[1] // 4
    share = quarter // 4
    for piece in range(4):
        turned = source[:, piece * quarter : (piece + 1) * quarter].T
        for inner in range(4):
            x, z, y = piece // 2, 2 * (piece % 2) + inner // 2, inner % 2
            left_t[index, x, y, z * share : (z + 1) * share] = turned[
                inner * share : (inner + 1) * share
            ]


def remote(source, target, send, recv, device):
    return pltpu.make_async_remote_copy(
        src_ref=source,
        dst_ref=target,
        send_sem=send,
        recv_sem=recv,
        device_id=device,
        device_id_type=MESH,
    )


def move(source, target, send, recv, device, is_self):
    @pl.when(is_self)
    def _():
        pltpu.make_async_copy(source, target, recv).start()

    @pl.when(jnp.logical_not(is_self))
    def _():
        remote(source, target, send, recv, device).start()


def return_copies(ref, out, send, recv):
    row, spot, core = place()
    head = 2 * lax.rem(spot, 4) + core
    owner = spot // 4
    copies = []
    for step in range(8):
        chip = lax.rem(spot + step, 8)
        is_self = (owner == core) if step == 0 else False
        parts = (ref.at[chip], out.at[head], send.at[step], recv.at[head], (row, chip, owner))
        copies.append((parts, is_self))
    return copies


def start_return(copies):
    for parts, is_self in copies:
        if is_self is False:
            remote(*parts).start()
        else:
            move(*parts, is_self)


def finish_return(copies, out, send, recv):
    row, spot, core = place()
    for head in range(8):
        remote(
            out.at[head], out.at[head], send.at[0], recv.at[head], (row, spot, 1 - core)
        ).wait_recv()
    for parts, is_self in copies:
        if is_self is False:
            remote(*parts).wait_send()
        else:

            @pl.when(jnp.logical_not(is_self))
            def _():
                remote(*parts).wait_send()


def tile_at(index, size):
    return pl.ds(pl.multiple_of(index * size, size), size)


def causal(scores):
    keys = lax.broadcasted_iota(jnp.int32, scores.shape, 0)
    queries = lax.broadcasted_iota(jnp.int32, scores.shape, 1)
    return jnp.where(keys <= queries, scores, masked_value)


def neighbours():
    row, spot, core = place()
    level, column = spot // 2, lax.rem(spot, 2)
    beside_x = (1 - row, spot, core)
    beside_y = (row, 2 * level + 1 - column, core)
    along_z = [(row, 2 * lax.rem(level + k, 4) + column, core) for k in (1, 2, 3)]
    return row, level, column, beside_x, beside_y, along_z


class Gather:
    def __init__(self, own, whole, start, width, piece, sems):
        self.own, self.whole = own.at[:, pl.ds(start, width)], whole
        self.start, self.width = start, width
        names = ("send_z", "recv_z", "send_x", "recv_x", "send_y", "recv_y", "send_d", "recv_d")
        for name, sem in zip(names + ("local",), sems):
            setattr(self, name, sem.at[piece])

    def block(self, x, z, y, half=None):
        cut = self.width * 7 // 12 // WIDE * WIDE
        start, width = self.start, self.width
        if half == 0:
            width = cut
        elif half == 1:
            start, width = start + cut, width - cut
        return self.whole.at[x, z, y, :, pl.ds(start, width)]

    def arrived(self, target, recv_sem):
        device = neighbours()[3]
        remote(target, target, self.send_x.at[0], recv_sem, device).wait_recv()

    def copy_z(self, z, up, own=False):
        row, level, column, beside_x, beside_y = neighbours()[:5]
        core = place()[2]
        target = level + 1 if up else level - 1
        block = self.block(row, z, column)
        return remote(
            self.own if own else block,
            block,
            self.send_z.at[int(up), z],
            self.recv_z.at[z],
            (row, 2 * target + column, core),
        )

    def copies_xy(self, z, own=False):
        row, level, column, beside_x, beside_y = neighbours()[:5]
        block = self.block(row, z, column)
        source = self.own if own else block
        return [
            remote(source, block, self.send_x.at[z], self.recv_x.at[z], beside_x),
            remote(source, block, self.send_y.at[z], self.recv_y.at[z], beside_y),
        ]

    def copies_diagonal(self, z):
        row, level, column, beside_x, beside_y = neighbours()[:5]
        by_y = self.block(1 - row, z, column, 1)
        by_x = self.block(row, z, 1 - column, 0)
        return [
            remote(by_y, by_y, self.send_d.at[0, z], self.recv_d.at[0, z], beside_y),
            remote(by_x, by_x, self.send_d.at[1, z], self.recv_d.at[1, z], beside_x),
        ]

    def own_copy(self):
        row, level, column = neighbours()[:3]
        return pltpu.make_async_copy(self.own, self.block(row, level, column), self.local)

    def each_at(self, hop, act):
        level = neighbours()[1]

        @pl.when(level >= hop)
        def _():
            act(level - hop, True)

        @pl.when(level + hop <= 3)
        def _():
            act(level + hop, False)

    def start_z(self, z, up, own=False):
        level = neighbours()[1]

        @pl.when(level < 3 if up else level > 0)
        def _():
            self.copy_z(z, up, own).start()

    def place_own(self):
        self.own_copy().start()

    def open(self):
        level = neighbours()[1]
        self.start_z(level, True, True)
        self.start_z(level, False, True)
        for copy in self.copies_xy(level, True):
            copy.start()

    def hop(self, hop):
        def act(z, up):
            row, level, column = neighbours()[:3]
            self.arrived(self.block(row, z, column), self.recv_z.at[z])
            self.start_z(z, up)
            for copy in self.copies_xy(z):
                copy.start()

        self.each_at(hop, act)

    def turn_diagonal(self, z):
        row, level, column = neighbours()[:3]
        by_y, by_x = self.copies_diagonal(z)
        self.arrived(self.block(1 - row, z, column), self.recv_x.at[z])
        by_y.start()
        self.arrived(self.block(row, z, 1 - column), self.recv_y.at[z])
        by_x.start()

    def diagonal(self, hop):
        if hop == 0:
            self.turn_diagonal(neighbours()[1])
        else:
            self.each_at(hop, lambda z, up: self.turn_diagonal(z))

    def finish(self):
        row, level, column = neighbours()[:3]
        self.own_copy().wait()
        for z in range(4):
            self.arrived(self.block(1 - row, z, 1 - column, 1), self.recv_d.at[0, z])
            self.arrived(self.block(1 - row, z, 1 - column, 0), self.recv_d.at[1, z])

    def close_z(self):
        level = neighbours()[1]

        def sent(z, up):
            @pl.when(level < 3 if up else level > 0)
            def _():
                self.copy_z(z, up).wait_send()

        sent(level, True)
        sent(level, False)
        for hop in range(1, 4):
            self.each_at(hop, sent)

    def close(self):
        self.close_z()
        for z in range(4):
            for copy in self.copies_xy(z) + self.copies_diagonal(z):
                copy.wait_send()


class PlaneGather(Gather):
    def plane(self, z):
        return self.whole.at[:, z, :, :, pl.ds(self.start, self.width)]

    def copy_z(self, z, up, own=False):
        row, level, column = neighbours()[:3]
        target = level + 1 if up else level - 1
        plane = self.plane(z)
        return remote(
            plane,
            plane,
            self.send_z.at[int(up), z],
            self.recv_z.at[z],
            (row, 2 * target + column, place()[2]),
        )

    def open(self):
        for copy in self.copies_xy(neighbours()[1], True):
            copy.start()

    def spread(self):
        row, level, column = neighbours()[:3]
        self.arrived(self.block(1 - row, level, 1 - column, 1), self.recv_d.at[0, level])
        self.arrived(self.block(1 - row, level, 1 - column, 0), self.recv_d.at[1, level])
        self.own_copy().wait()
        self.start_z(level, True)
        self.start_z(level, False)

    def hop(self, hop):
        def act(z, up):
            self.arrived(self.plane(z), self.recv_z.at[z])
            self.start_z(z, up)

        self.each_at(hop, act)

    def finish(self):
        pass

    def close(self):
        level = neighbours()[1]
        self.close_z()
        for copy in self.copies_xy(level) + self.copies_diagonal(level):
            copy.wait_send()


def gather_sems(pieces):
    dma = pltpu.SemaphoreType.DMA
    shapes = [(2, 4), (4,), (4,), (4,), (4,), (4,), (2, 4), (2, 4), ()]
    return [dma((pieces,) + shape) for shape in shapes]


AT_BEGIN, AT_GAINS, AT_PAIRS, AT_QUERIES, AT_HEADS, AT_KEYS, AT_ALL, AT_SORT = 0, 1, 2, 3, 4, 5, 6, 7
AT_RETURN, AT_MIXED, AT_OUT, AT_NORM, AT_GROUP, AT_TILE, AT_FEED = 8, 9, 10, 11, 12, 16, 24
PUMPS = {
    AT_BEGIN: (1, 10, 4, 2, 3, 5, 7, 6, 11, 12, 13, 14),
    AT_GAINS: (20,),
    AT_GROUP + 2: (15, 17),
    AT_GROUP + 3: (16, 70),
    AT_QUERIES: (21, 30),
    AT_GROUP + 0: (50,),
    AT_GROUP + 1: (22,),
    AT_HEADS: (74, 40, 31, 60, 23),
    AT_KEYS: (34, 75),
    AT_ALL: (32, 24, 35, 44),
    AT_TILE + 0: (41, 25),
    AT_TILE + 2: (33, 26, 61, 42, 71),
    AT_TILE + 3: (27, 51),
    AT_RETURN: (36, 37, 43, 52, 45, 55, 72, 47, 54, 46),
    AT_MIXED: (64,),
    AT_OUT: (53,),
    AT_NORM: (56, 62),
    AT_FEED + 1: (63, 57),
    AT_FEED + 3: (65, 66, 67),
    AT_FEED + 5: (73,),
}


def forward_kernel(
    tokens,
    positions,
    freqs,
    gain_one,
    gain_two,
    w_query,
    w_key,
    w_value,
    w_out_t,
    w_gate,
    w_up,
    w_down_t,
    cotangent,
    near,
    far,
    normed_out,
    q_out,
    k_out,
    v_out,
    mixed_t_out,
    lse_out,
    mixed_low_out,
    middle_out,
    second_out,
    right_out,
    gains_out,
    tables_out,
    left_out,
    order,
    ids_flat,
    ids_in,
    near_own,
    far_own,
    unit,
    normed,
    tables,
    weight,
    gain_message,
    gain_all,
    gain_columns,
    gain_rows,
    left_t,
    q_heads,
    kv_heads,
    q_slots,
    kv_slots,
    q_t,
    keys,
    v_t,
    mixed_t,
    lse,
    mixed,
    mixed_slots,
    mixed_heads,
    mixed_low,
    out_weight,
    part,
    part_other,
    second,
    cot,
    right,
    feed_weight,
    ids_all,
    ids,
    load_own,
    send_ids,
    recv_ids,
    load_ids,
    send_gain,
    recv_gain,
    load_w,
    load_out,
    load_feed,
    load_cot,
    save_right,
    saves,
    send_q,
    recv_q,
    send_kv,
    recv_kv,
    send_x,
    recv_x,
    send_m,
    recv_m,
    send_p,
    recv_p,
    *sems,
):
    row, spot, core = place()
    low, full = jnp.bfloat16, jnp.float32
    rows, width = tokens.shape
    share = near_own.shape[0]
    length = 8 * rows
    runs, tiles = length // RUN, length // TILE
    per_device = rows // RUN
    halves = TILE // RUN
    quarter = 4 * share
    sibling = (row, spot, 1 - core)
    out_width = w_out_t.shape[1]
    qkv_width = 16 * HEAD

    near_loads, far_loads, start = [], [], 0
    for ref in (w_query, w_key, w_value, w_out_t):
        target = near_own.at[:, pl.ds(start, ref.shape[1])]
        near_loads.append(pltpu.make_async_copy(ref, target, load_own.at[len(near_loads)]))
        start += ref.shape[1]
    for index, ref in enumerate((w_gate, w_up, w_down_t)):
        for piece in range(4):
            source = ref.at[:, pl.ds(piece * FEED, FEED)]
            target = far_own.at[:, pl.ds((3 * piece + index) * FEED, FEED)]
            far_loads.append(
                pltpu.make_async_copy(source, target, load_own.at[4 + 4 * index + piece])
            )
    for copy in near_loads + far_loads:
        copy.start()
    load_cotangent = pltpu.make_async_copy(cotangent, cot, load_cot)
    load_cotangent.start()
    half = qkv_width // 2
    pairs = Gather(near_own, near, half, half, 0, sems)
    first = Gather(near_own, near, 0, half, 1, sems)
    outer = Gather(near_own, near, qkv_width, out_width, 2, sems)
    feeds = [Gather(far_own, far, 3 * FEED * p, 3 * FEED, 3 + p, sems) for p in range(3)]
    feeds.append(Gather(far_own, far, 9 * FEED, FEED, 6, sems))
    plane = PlaneGather(far_own, far, 10 * FEED, 2 * FEED, 7, sems)
    gathers = [pairs, first, outer] + feeds + [plane]

    def pump(place):
        for what in PUMPS.get(place, ()):
            gather, act = gathers[what // 10], what % 10
            if act == 0:
                gather.open()
            elif act < 4:
                gather.hop(act)
            elif gather is plane and act == 5:
                gather.spread()
            else:
                gather.diagonal(act - 4)

    gain_message[...] = jnp.zeros_like(gain_message)
    gain_message[0:1, :share] = gain_one[...].astype(full)
    gain_message[1:2, :share] = gain_two[...].astype(full)
    for copy in near_loads:
        copy.wait()
    greet(group_others())
    pairs.open()
    for gather in (pairs, first, outer):
        gather.place_own()

    gain_copies, gain_from = exchange_messages(
        lambda shard: gain_message, gain_all, send_gain, recv_gain
    )
    for copy in gain_copies:
        copy.start()
    gain_all[own_shard()] = gain_message[...]

    lane = lax.broadcasted_iota(jnp.int32, (8, WIDE), 1)
    ids_in[...] = jnp.zeros_like(lane)
    for run in range(per_device):
        start_at = positions[0:1, run * RUN : run * RUN + 1]
        ids_in[...] = jnp.where(lane == run, lax.div(start_at, RUN), ids_in[...])
    for shift in range(1, 8):
        remote(
            ids_in,
            ids_all.at[spot],
            send_ids.at[shift],
            recv_ids.at[shift],
            (row, lax.rem(spot + shift, 8), core),
        ).start()
    ids_all[spot] = ids_in[...]

    for copy in far_loads:
        copy.wait()
    for gather in feeds + [plane]:
        gather.place_own()
    chunk = rows // 8

    def unit_block(index, carry):
        cut = tile_at(index, chunk)
        values = tokens[cut].astype(full)
        inverse = lax.rsqrt(jnp.mean(values * values, axis=-1, keepdims=True) + epsilon)
        unit[cut] = values * inverse
        return carry

    lax.fori_loop(0, 8, unit_block, 0)
    angles = freqs[...] * positions[...].astype(full)
    tables[0] = jnp.cos(angles)
    tables[1] = jnp.sin(angles)

    pump(AT_BEGIN)
    for shift in range(1, 8):
        remote(
            ids_in,
            ids_all.at[lax.rem(spot + 8 - shift, 8)],
            send_ids.at[shift],
            recv_ids.at[shift],
            (row, lax.rem(spot + shift, 8), core),
        ).wait_recv()
    pltpu.make_async_copy(ids_all, ids, load_ids).start()
    pairs.finish()

    width = near.shape[3] * 16

    def load_group(group):
        lanes = pl.ds(group * 4 * HEAD, 4 * HEAD)
        return pltpu.make_async_copy(
            near.at[:, :, :, :, lanes], weight.at[group % 2], load_w.at[group % 2]
        )

    load_out_weight = pltpu.make_async_copy(
        near.at[:, :, :, :, pl.ds(qkv_width, out_width)], out_weight, load_out
    )
    load_group(2).start()
    load_group(3).start()
    for wait in gain_from:
        wait()
    for shard in range(16):
        gain_columns[shard * share : (shard + 1) * share] = gain_all[shard].T[:share]
    gain_rows[...] = gain_columns[...].T
    normed[...] = (unit[...] * gain_rows[0:1]).astype(low)
    pump(AT_GAINS)

    def project(group):
        load_group(group).wait()
        proj = dot_f32(normed[...], weight[group % 2].reshape(width, 4 * HEAD)).T
        for head in range(4):
            front = proj[head * HEAD : head * HEAD + HALF]
            back = proj[head * HEAD + HALF : (head + 1) * HEAD]
            if group < 3:
                front, back = (
                    front * tables[0] - back * tables[1],
                    back * tables[0] + front * tables[1],
                )
            for start, value in ((0, front.astype(low)), (HALF, back.astype(low))):
                for run in range(per_device):
                    piece = value[:, run * RUN : (run + 1) * RUN]
                    if group < 2:
                        q_heads[4 * group + head, run, start : start + HALF] = piece
                    else:
                        kv_heads[head, group - 2, run, start : start + HALF] = piece
        pump(AT_GROUP + group)

    project(2)
    project(3)

    outgoing = []
    for step in range(4):
        slot = lax.rem(spot + step, 4)
        chip = 4 * core + slot
        for other in range(2):
            is_self = jnp.logical_and(chip == spot, core == other)
            device = (row, chip, other)
            kv_parts = (
                kv_heads.at[slot, :, other],
                kv_slots.at[spot, :, other],
                send_kv.at[step, other],
                recv_kv.at[spot],
                device,
            )
            q_parts = (
                q_heads.at[2 * slot + other],
                q_slots.at[spot],
                send_q.at[step, other],
                recv_q.at[spot],
                device,
            )
            outgoing.append((kv_parts, is_self))
            outgoing.append((q_parts, is_self))
    for parts, is_self in outgoing[0::2]:
        move(*parts, is_self)
    pump(AT_PAIRS)
    first.finish()
    load_group(0).start()
    load_group(1).start()
    pump(AT_QUERIES)
    project(0)
    project(1)
    for parts, is_self in outgoing[1::2]:
        move(*parts, is_self)
    pump(AT_HEADS)

    def hand_on(source):
        block = kv_slots.at[source, :, core]
        return remote(block, block, send_x.at[source], recv_x.at[source], sibling)

    for step in range(8):
        source = lax.rem(spot + step, 8)
        block = kv_slots.at[source, :, core]
        remote(block, block, send_x.at[source], recv_kv.at[source], sibling).wait_recv()
        hand_on(source).start()
    pump(AT_KEYS)
    for step in range(8):
        remote(
            q_slots.at[step], q_slots.at[step], send_x.at[step], recv_q.at[step], sibling
        ).wait_recv()
        hand_on(step).wait()
    pump(AT_ALL)

    pltpu.make_async_copy(ids_all, ids, load_ids).wait()

    def find_run(index, carry):
        device, piece = 0, 0
        for run in range(runs):
            here = ids[run // per_device, 0, run % per_device] == index
            device = jnp.where(here, run // per_device, device)
            piece = jnp.where(here, run % per_device, piece)
        order[index, 0] = device
        order[index, 1] = piece
        found = ids[index // per_device, 0, index % per_device]
        order[runs + index, 0] = lax.div(found, per_device)
        order[runs + index, 1] = lax.rem(found, per_device)
        ids_flat[index] = found
        return carry

    lax.fori_loop(0, runs, find_run, 0)

    def sort_run(index, carry):
        device, piece = order[index, 0], order[index, 1]
        cols = tile_at(index, RUN)
        q_t[:, cols] = q_slots[device, piece]
        keys[index] = kv_slots[device, 0, piece].T
        v_t[:, cols] = kv_slots[device, 1, piece]
        return carry

    lax.fori_loop(0, runs, sort_run, 0)
    pump(AT_SORT)
    scale = HEAD ** (-0.5) * LOG2_E

    def query_pair(pair, carry):
        def step(half, scores, block, peak, total, mix):
            high = jnp.maximum(peak, jnp.max(scores, axis=0, keepdims=True))
            decay = jnp.exp2(peak - high)
            weights = jnp.exp2(scores - high)
            total = total * decay + jnp.sum(weights, axis=0, keepdims=True)
            mix = mix * decay + dot_f32(v_t[:, tile_at(block, TILE)], weights.astype(low))
            return high, total, mix

        def scores_of(half, block):
            held = keys[pl.ds(block * halves, halves)].reshape(TILE, HEAD)
            return dot_f32(held, q_t[:, tile_at(2 * pair + half, TILE)]) * scale

        def full_block(block, states):
            scores = [scores_of(half, block) for half in range(2)]
            return tuple(step(half, scores[half], block, *states[half]) for half in range(2))

        state = (
            jnp.full((1, TILE), masked_value, full),
            jnp.zeros((1, TILE), full),
            jnp.zeros((HEAD, TILE), full),
        )
        start = 2 * pair
        scores = causal(scores_of(0, start)), scores_of(1, start)
        states = tuple(step(half, scores[half], start, *state) for half in range(2))
        last = step(1, causal(scores_of(1, start + 1)), start + 1, *states[1])
        states = lax.fori_loop(0, start, full_block, (states[0], last))
        for half in range(2):
            peak, total, mix = states[half]
            index = 2 * pair + half
            cols = tile_at(index, TILE)
            mix = mix / total
            mixed_t[:, cols] = mix
            lse[:, cols] = peak + jnp.log2(total)
            for run in range(halves):
                cut = mix[:, run * RUN : (run + 1) * RUN]
                mixed[index * halves + run] = cut.astype(low)
        for place in range(tiles // 2):

            @pl.when(pair == place)
            def _():
                pump(AT_TILE + place)

        return carry

    lax.fori_loop(0, tiles // 2, query_pair, 0)

    def unsort_run(run, carry):
        index = ids[run // per_device, 0, run % per_device]
        mixed_slots[run // per_device, run % per_device] = mixed[index]
        return carry

    lax.fori_loop(0, runs, unsort_run, 0)
    copies = return_copies(mixed_slots, mixed_heads, send_m, recv_m)
    start_return(copies)
    early_saves = [
        pltpu.make_async_copy(source, target, saves.at[index])
        for index, (source, target) in enumerate(
            [
                (normed, normed_out),
                (q_t, q_out),
                (keys, k_out),
                (v_t, v_out),
                (mixed_t, mixed_t_out),
                (lse, lse_out),
                (gain_rows, gains_out),
                (tables, tables_out),
            ]
        )
    ]
    for copy in early_saves:
        copy.start()
    pump(AT_RETURN)
    outer.finish()
    load_out_weight.start()
    finish_return(copies, mixed_heads, send_m, recv_m)
    pump(AT_MIXED)

    load_out_weight.wait()
    for run in range(per_device):
        side = mixed_heads[:, run].reshape(8 * HEAD, RUN)
        mixed_low[run * RUN : (run + 1) * RUN] = side.T

    def pair_copy(index):
        cut = pl.ds(index * quarter, quarter)
        return remote(
            part.at[:, cut], part_other.at[:, cut], send_p.at[index], recv_p.at[index], sibling
        )

    for index in range(4):
        block = out_weight[index // 2, 2 * (index % 2) : 2 * (index % 2) + 2]
        term = contract_cols(mixed_low[...], block.reshape(quarter, out_width))
        part[:, index * quarter : (index + 1) * quarter] = term.astype(low)
        pair_copy(index).start()
    pump(AT_OUT)
    load_cotangent.wait()
    for index in range(4):
        pair_copy(index).wait()
    chunk = rows // 8

    def norm_block(index, carry):
        cut = tile_at(index, chunk)
        sums = part[cut].astype(full) + part_other[cut].astype(full)
        values = tokens[cut].astype(full) + sums
        unit[cut] = values
        inverse = lax.rsqrt(jnp.mean(values * values, axis=-1, keepdims=True) + epsilon)
        second[cut] = (values * inverse * gain_rows[1:2]).astype(low)
        return carry

    lax.fori_loop(0, 8, norm_block, 0)
    late_saves = [
        pltpu.make_async_copy(source, target, saves.at[8 + index])
        for index, (source, target) in enumerate(
            [(mixed_low, mixed_low_out), (unit, middle_out), (second, second_out)]
        )
    ]
    for copy in late_saves:
        copy.start()
    pump(AT_NORM)

    def load_feed_weight(index, kind):
        piece, half = index // 2, lax.rem(index, 2)
        start = (3 * piece + kind) * FEED + half * PIECE
        lanes = pl.ds(pl.multiple_of(start, PIECE), PIECE)
        return pltpu.make_async_copy(
            far.at[:, :, :, :, lanes], feed_weight.at[half, kind], load_feed.at[half, kind]
        )

    def load_half(index):
        for kind in range(3):
            load_feed_weight(index, kind).start()

    def save_piece(piece):
        lanes = pl.ds(piece * 3 * FEED, 3 * FEED)
        return pltpu.make_async_copy(
            right.at[:, lanes], right_out.at[:, lanes], save_right.at[piece]
        )

    def feed_block(index, carry):
        piece, half = index // 2, lax.rem(index, 2)
        for when in range(3):

            @pl.when(index == (2 * when + 1 if when < 2 else 6))
            def _():
                feeds[when + 1].finish()

        @pl.when(index == 0)
        def _():
            load_half(0)

        @pl.when(index == 6)
        def _():
            load_half(6)

        @pl.when(jnp.logical_and(index != 5, index != 7))
        def _():
            load_half(index + 1)

        values = []
        for kind, left in enumerate((second, second, cot)):
            load_feed_weight(index, kind).wait()
            values.append(dot_f32(left[...], feed_weight[half, kind].reshape(width, PIECE)))
        gate, up, grad_hidden = values
        sigmoid = jax.nn.sigmoid(gate)
        silu = gate * sigmoid
        grad_gate = grad_hidden * up * sigmoid * (1.0 + gate * (1.0 - sigmoid))
        for when, source in ((1, second), (3, cot)):

            @pl.when(index == when)
            def _():
                turn_left(left_t, when % 3, source)

        for kind, value in enumerate((grad_gate, grad_hidden * silu, silu * up)):
            start = (3 * piece + kind) * FEED + half * PIECE
            right[:, pl.ds(pl.multiple_of(start, PIECE), PIECE)] = value.astype(low)

        for when in range(8):

            @pl.when(index == when)
            def _():
                pump(AT_FEED + when)

        for when in range(4):

            @pl.when(index == 2 * when + 1)
            def _():
                save_piece(when).start()

        return carry

    feeds[0].finish()
    lax.fori_loop(0, 8, feed_block, 0)
    save_left = pltpu.make_async_copy(left_t, left_out, saves.at[11])
    save_left.start()
    for gather in gathers:
        gather.close()
    for parts, is_self in outgoing:

        @pl.when(jnp.logical_not(is_self))
        def _():
            remote(*parts).wait_send()

    for shift in range(1, 8):
        remote(
            ids_in,
            ids_all.at[spot],
            send_ids.at[shift],
            recv_ids.at[shift],
            (row, lax.rem(spot + shift, 8), core),
        ).wait_send()
    for copy in gain_copies:
        copy.wait_send()
    for copy in early_saves + late_saves + [save_left] + [save_piece(piece) for piece in range(4)]:
        copy.wait()


def forward(
    tokens,
    positions,
    gain_one,
    gain_two,
    w_query,
    w_key,
    w_value,
    w_out_t,
    w_gate,
    w_up,
    w_down_t,
    cotangent,
):
    dma = pltpu.SemaphoreType.DMA
    vmem = pltpu.VMEM
    low, full = jnp.bfloat16, jnp.float32
    rows, width = tokens.shape
    share, hidden_width = w_gate.shape
    out_width = w_out_t.shape[1]
    near_width = 16 * HEAD + out_width
    length = 8 * rows
    per_device = rows // RUN
    heads = (8, per_device, HEAD, RUN)
    both = (2, per_device, HEAD, RUN)
    by_run = (length // RUN, RUN, HEAD)
    flat = (HEAD, length)
    smem_spec = pl.BlockSpec(memory_space=pltpu.SMEM)
    shape = jax.ShapeDtypeStruct
    return pl.pallas_call(
        forward_kernel,
        in_specs=[vmem_spec()] * 5 + [any_spec()] * 8,
        out_specs=[any_spec()] * 15 + [smem_spec] * 2,
        out_shape=[
            shape((2, 4, 2, share, near_width), low),
            shape((2, 4, 2, share, 3 * hidden_width), low),
            shape((rows, width), low),
            shape(flat, low),
            shape(by_run, low),
            shape(flat, low),
            shape(flat, full),
            shape((1, length), full),
            shape((rows, out_width), low),
            shape((rows, width), full),
            shape((rows, width), low),
            shape((rows, 3 * hidden_width), low),
            shape((8, width), full),
            shape((2, HALF, rows), full),
            shape((2, 2, 2, 4 * share, rows), low),
            shape((2 * length // RUN, 2), jnp.int32),
            shape((length // RUN,), jnp.int32),
        ],
        scratch_shapes=[
            vmem((8, WIDE), jnp.int32),
            vmem((share, near_width), low),
            vmem((share, 3 * hidden_width), low),
            vmem((rows, width), full),
            vmem((rows, width), low),
            vmem((2, HALF, rows), full),
            vmem((2, 2, 4, 2, share, 4 * HEAD), low),
            vmem((8, WIDE), full),
            vmem((16, 8, WIDE), full),
            vmem((width, 8), full),
            vmem((8, width), full),
            vmem((2, 2, 2, 4 * share, rows), low),
            vmem(heads, low),
            vmem((4,) + both, low),
            vmem(heads, low),
            vmem((8,) + both, low),
            vmem(flat, low),
            vmem(by_run, low),
            vmem(flat, low),
            vmem(flat, full),
            vmem((1, length), full),
            vmem((length // RUN, HEAD, RUN), low),
            vmem(heads, low),
            vmem(heads, low),
            vmem((rows, out_width), low),
            vmem((2, 4, 2, share, out_width), low),
            vmem((rows, width), low),
            vmem((rows, width), low),
            vmem((rows, width), low),
            vmem((rows, width), low),
            vmem((rows, 3 * hidden_width), low),
            vmem((2, 3, 2, 4, 2, share, PIECE), low),
            vmem((8, 8, WIDE), jnp.int32),
            pltpu.SMEM((8, 8, WIDE), jnp.int32),
            dma((16,)),
            dma((8,)),
            dma((8,)),
            dma(()),
            dma((16,)),
            dma((16,)),
            dma((2,)),
            dma(()),
            dma((2, 3)),
            dma(()),
            dma((4,)),
            dma((12,)),
            dma((4, 2)),
            dma((8,)),
            dma((4, 2)),
            dma((8,)),
            dma((8,)),
            dma((8,)),
            dma((8,)),
            dma((8,)),
            dma((4,)),
            dma((4,)),
        ]
        + gather_sems(8),
        compiler_params=pltpu.CompilerParams(
            collective_id=1, has_side_effects=True, vmem_limit_bytes=VMEM_LIMIT
        ),
        name="forward",
    )(
        tokens,
        positions,
        lane_freqs(),
        gain_one,
        gain_two,
        w_query,
        w_key,
        w_value,
        w_out_t,
        w_gate,
        w_up,
        w_down_t,
        cotangent,
    )


SECOND, THIRD, LAST = 2, 4, 5


class Reduce:
    def __init__(self, n, changes, refs):
        (
            self.left_t,
            self.right,
            self.own,
            self.out,
            self.save,
            self.send_one,
            self.recv_one,
            self.send_two,
            self.recv_two,
            self.kept,
            self.recv_three,
            self.ss_one,
            self.rs_one,
            self.ss_two,
            self.rs_two,
            self.ss_three,
            self.rs_three,
        ) = refs
        self.n, self.changes = n, changes
        self.share = self.own.shape[1]

    def columns(self, step, kind):
        held = self.right.shape[1] // (2 * PIECE)
        start = lax.rem(step, held) * 2 * PIECE + kind * PIECE
        return pl.ds(pl.multiple_of(start, PIECE), PIECE)

    def each_save(self, step, act):
        slot = lax.rem(step, 2)
        near_at = self.changes[0]

        def copies(cuts):
            for index, (ref, start, lanes) in enumerate(cuts):
                source = self.own.at[slot, :, lanes]
                target = ref.at[:, pl.ds(start, lanes.size)]
                act(pltpu.make_async_copy(source, target, self.save.at[slot, index]))

        for kind in range(3):

            @pl.when(jnp.logical_and(step < near_at, lax.rem(step, 3) == kind))
            def _():
                start = pl.multiple_of(step // 3 * 2 * PIECE, 2 * PIECE)
                copies([(self.out[kind], start, pl.ds(0, 2 * PIECE))])

        for index in range(self.n - near_at):
            first, past = index * 2 * PIECE, (index + 1) * 2 * PIECE
            cuts, at = [], 0
            for ref in self.out[3:]:
                low, high = max(first, at), min(past, at + ref.shape[1])
                if low < high:
                    cuts.append((ref, low - at, pl.ds(low - first, high - low)))
                at += ref.shape[1]

            @pl.when(step == near_at + index)
            def _():
                copies(cuts)

    def product(self, step, kind, x, y):
        left = jnp.where(lax.rem(step, 3) == 2, 0, 1)
        left = jnp.where(step >= self.changes[0], 2, left)
        left = jnp.where(step >= self.changes[1], 0, left)
        term = jnp.dot(
            self.left_t[left, x, y],
            self.right[:, self.columns(step, kind)],
            preferred_element_type=jnp.float32,
        )
        return term

    def x_first(self, step, kind):
        return 1 if kind == 0 else jnp.where(lax.rem(step, 5) == 4, 1, 0)

    def beside(self, by_x):
        row, level, column = neighbours()[:3]
        core = place()[2]
        other_row = by_x * (1 - row) + (1 - by_x) * row
        other_column = by_x * column + (1 - by_x) * (1 - column)
        return (other_row, 2 * level + other_column, core)

    def first_copy(self, step, kind):
        out, into = lax.rem(step, 3), lax.rem(step, 6)
        return remote(
            self.send_one.at[out, kind],
            self.recv_one.at[into, kind],
            self.ss_one.at[out, kind],
            self.rs_one.at[into, kind],
            self.beside(self.x_first(step, kind)),
        )

    def second_copy(self, step, kind):
        out, into = lax.rem(step, 3), lax.rem(step, 6)
        return remote(
            self.send_two.at[out, kind],
            self.recv_two.at[into, kind],
            self.ss_two.at[out, kind],
            self.rs_two.at[into, kind],
            self.beside(1 - self.x_first(step, kind)),
        )

    def third_copy(self, step, kind, k):
        row, level, column, beside_x, beside_y, along_z = neighbours()
        target = lax.rem(level + k + 1, 4)
        out, into = lax.rem(step, 4), lax.rem(step, 4)
        return remote(
            self.kept.at[out, kind, pl.ds(pl.multiple_of(target * self.share, 16), self.share)],
            self.recv_three.at[into, kind, k],
            self.ss_three.at[out, kind, k],
            self.rs_three.at[into, kind, k],
            along_z[k],
        )

    def pieces(self, step, act):
        act(0)

        @pl.when(step < self.n - 1)
        def _():
            act(1)

    def first(self, step):
        row, level, column = neighbours()[:3]
        slot = lax.rem(step, 3)

        def act(kind):
            by_x = self.x_first(step, kind)
            for half in range(2):
                x = by_x * (1 - row) + (1 - by_x) * half
                y = by_x * half + (1 - by_x) * (1 - column)
                self.send_one[slot, kind, half] = self.product(step, kind, x, y).astype(
                    jnp.bfloat16
                )
            self.first_copy(step, kind).start()

        self.pieces(step, act)

    def second(self, step):
        row, level, column = neighbours()[:3]
        slot, came, keep = lax.rem(step, 3), lax.rem(step, 6), lax.rem(step, 4)
        self.pieces(step, lambda kind: self.first_copy(step, kind).wait())

        def act(kind):
            by_x = self.x_first(step, kind)
            x = by_x * row + (1 - by_x) * (1 - row)
            y = by_x * (1 - column) + (1 - by_x) * column
            arrived = self.recv_one.at[came, kind]
            mine = by_x * column + (1 - by_x) * row
            away = self.product(step, kind, x, y) + arrived[1 - mine].astype(jnp.float32)
            self.send_two[slot, kind] = away.astype(jnp.bfloat16)
            here = self.product(step, kind, row, column) + arrived[mine].astype(jnp.float32)
            self.kept[keep, kind] = here.astype(jnp.bfloat16)

        self.pieces(step, act)
        self.pieces(step, lambda kind: self.second_copy(step, kind).start())

    def third(self, step):
        came, keep = lax.rem(step, 6), lax.rem(step, 4)

        def act(kind):
            self.second_copy(step, kind).wait()
            here = self.kept[keep, kind].astype(jnp.float32) + self.recv_two[came, kind].astype(
                jnp.float32
            )
            self.kept[keep, kind] = here.astype(jnp.bfloat16)
            for k in range(3):
                self.third_copy(step, kind, k).start()

        self.pieces(step, act)

    def last(self, step):
        level = neighbours()[1]
        came, keep = lax.rem(step, 4), lax.rem(step, 4)
        mine = pl.ds(pl.multiple_of(level * self.share, 16), self.share)

        @pl.when(step >= 2)
        def _():
            self.each_save(step - 2, lambda copy: copy.wait())

        def act(kind):
            total = self.kept[keep, kind, mine].astype(jnp.float32)
            for k in range(3):
                self.third_copy(step, kind, k).wait()
                total = total + self.recv_three[came, kind, k].astype(jnp.float32)
            self.own[lax.rem(step, 2), :, kind * PIECE : (kind + 1) * PIECE] = total

        self.pieces(step, act)
        self.each_save(step, lambda copy: copy.start())

    def turn(self, step):
        for stage, lag in (
            (self.first, 0),
            (self.second, SECOND),
            (self.third, THIRD),
            (self.last, LAST),
        ):

            @pl.when(jnp.logical_and(step >= lag, step < self.n + lag))
            def _():
                stage(step - lag)


def backward_kernel(
    order,
    ids,
    q_in,
    k_in,
    v_in,
    mixed_t_in,
    lse_in,
    cotangent,
    left_in,
    normed_in,
    right_in,
    mixed_low,
    middle,
    near,
    far,
    tokens,
    gains_in,
    tables,
    input_grad,
    layer_out,
    gate_grad,
    up_grad,
    down_grad,
    query_grad,
    key_grad,
    value_grad,
    out_grad,
    gain_out,
    q,
    q_t,
    k,
    k_t,
    v,
    d_own,
    d_slots,
    d,
    d_t,
    dq_t,
    lse,
    delta,
    dk,
    dv,
    dq_slots,
    dkv_sorted,
    dkv_slots,
    dkv_other,
    dq_own,
    dkv_own,
    weight,
    middle_ring,
    input_ring,
    part,
    part_other,
    total,
    staged,
    grad_mid,
    gain_two_grad,
    left_t,
    right,
    gain_columns,
    gain_messages,
    gain_all,
    own,
    send_one,
    recv_one,
    send_two,
    recv_two,
    kept,
    recv_three,
    loads,
    load_first,
    send_gain,
    recv_gain,
    load_left_sem,
    load_w,
    load_ring,
    save_rows,
    save_sem,
    send_d,
    recv_d,
    send_q,
    recv_q,
    send_x,
    recv_x,
    send_k,
    recv_k,
    send_p,
    recv_p,
    save,
    *sems,
):
    row, spot, core = place()
    low, full = jnp.bfloat16, jnp.float32
    rows, width = staged.shape
    length = 8 * rows
    runs, tiles = length // RUN, length // TILE
    per_device = rows // RUN
    halves = TILE // RUN
    share = width // 16
    quarter = 4 * share
    sibling = (row, spot, 1 - core)
    qkv_width = 16 * HEAD
    out_width = mixed_low.shape[1]
    near_at = right_in.shape[1] // (2 * PIECE)
    n = near_at + (qkv_width + out_width + PIECE) // (2 * PIECE)
    grads = (gate_grad, up_grad, down_grad, query_grad, key_grad, value_grad, out_grad)
    changes = (near_at, near_at + qkv_width // (2 * PIECE))
    sums = Reduce(
        n,
        changes,
        (left_t, right, own, grads, save)
        + (send_one, recv_one, send_two, recv_two, kept, recv_three)
        + sems,
    )

    def stage(source):
        return pltpu.make_async_copy(source, staged, load_left_sem)

    early_loads = [
        pltpu.make_async_copy(source, target, loads.at[index])
        for index, (source, target) in enumerate(
            [
                (q_in, q_t),
                (k_in, k),
                (v_in, d_t),
                (mixed_t_in, dq_t),
                (lse_in, lse),
                (middle, total),
            ]
        )
    ]

    first_loads = [
        pltpu.make_async_copy(left_in, left_t.at[pl.ds(0, 2)], load_first.at[4])
    ] + [
        pltpu.make_async_copy(
            right_in.at[:, pl.ds(3 * FEED * piece, 3 * FEED)],
            right.at[:, pl.ds(3 * FEED * piece, 3 * FEED)],
            load_first.at[piece],
        )
        for piece in range(4)
    ]


    def load_block(index, piece, part_of, start):
        lanes = pl.ds(3 * FEED * piece + start + part_of * PIECE, PIECE)
        levels = pl.ds(2 * lax.rem(index, 2), 2)
        return pltpu.make_async_copy(
            far.at[index // 2, levels, :, :, lanes], held_block(piece, part_of), load_w.at[piece]
        )

    def held_block(piece, part_of):
        levels = pl.ds(2 * (part_of % 2), 2)
        return weight.at[piece, part_of // 2, levels, :, :, pl.ds(0, PIECE)]

    def load_blocks(index, piece, start, parts):
        for part_of in range(parts):
            load_block(index, piece, part_of, start).start()

    def row_products(start, parts, landing):
        def block(index, carry):
            term = jnp.zeros((rows, quarter), full)
            for piece in range(4):
                for part_of in range(parts):
                    load_block(index, piece, part_of, start).wait()
                for part_of in range(parts):
                    at = 3 * FEED * piece + start + part_of * PIECE
                    term = term + contract_cols(
                        right[:, at : at + PIECE],
                        held_block(piece, part_of)[...].reshape(quarter, PIECE),
                    )

                @pl.when(index + 1 < 4)
                def _():
                    load_blocks(index + 1, piece, start, parts)

            part[:, tile_at(index, quarter)] = term.astype(low)
            pair_copy(index, landing).start()
            return carry

        lax.fori_loop(0, 4, block, 0)

    def pair_copy(index, landing):
        cut = pl.ds(pl.multiple_of(index * quarter, quarter), quarter)
        return remote(
            part.at[:, cut],
            part_other.at[landing, :, cut],
            send_p.at[index],
            recv_p.at[landing, index],
            sibling,
        )

    def second_back():
        row_products(0, 4, 0)
        for index in range(2):
            load_out_weight(index).start()

    def load_out_weight(index):
        lanes = pl.ds(qkv_width + index * 4 * HEAD, 4 * HEAD)
        return pltpu.make_async_copy(
            near.at[:, :, :, :, lanes], weight.at[index], load_w.at[index]
        )

    d_copies = []
    for step in range(4):
        slot = lax.rem(spot + step, 4)
        chip = 4 * core + slot
        for other in range(2):
            parts = (
                d_own.at[2 * slot + other],
                d_slots.at[spot],
                send_d.at[step, other],
                recv_d.at[spot],
                (row, chip, other),
            )
            d_copies.append((parts, jnp.logical_and(chip == spot, core == other)))

    def middle_back():
        for index in range(4):
            pair_copy(index, 0).wait()
        early_loads[5].wait()
        stage(cotangent).wait()
        chunk = rows // 8

        def block(index, gain_grad):
            cut = tile_at(index, chunk)
            grad = part[cut].astype(full) + part_other[0, cut].astype(full)
            values = total[cut]
            inverse = lax.rsqrt(jnp.mean(values * values, axis=-1, keepdims=True) + epsilon)
            unit = values * inverse
            scaled = grad * gains_in[1:2]
            mean = jnp.mean(scaled * unit, axis=-1, keepdims=True)
            result = staged[cut].astype(full) + inverse * (scaled - unit * mean)
            total[cut] = result
            grad_mid[cut] = result.astype(low)
            return gain_grad + jnp.sum(grad * unit, axis=0, keepdims=True)

        gain_two_grad[...] = lax.fori_loop(0, 8, block, jnp.zeros((1, width), full))
        for index in range(2):
            load_out_weight(index).wait()
            grad = dot_f32(grad_mid[...], weight[index].reshape(width, 4 * HEAD)).T.astype(low)
            for head in range(4):
                for run in range(per_device):
                    d_own[4 * index + head, run] = grad[
                        head * HEAD : (head + 1) * HEAD, run * RUN : (run + 1) * RUN
                    ]
        for parts, is_self in d_copies:
            move(*parts, is_self)


    def prepare():
        for copy in early_loads[:5]:
            copy.wait()
        for index in range(tiles):
            cut = pl.ds(index * TILE, TILE)
            q[cut] = q_t[:, cut].T
            k_t[:, cut] = k[halves * index : halves * (index + 1)].reshape(TILE, HEAD).T
            v[cut] = d_t[:, cut].T

    def take_cotangents():
        for index in range(8):
            remote(
                d_slots.at[index], d_slots.at[index], send_d.at[0, 0], recv_d.at[index], sibling
            ).wait_recv()

        def sort_run(index, carry):
            cols = tile_at(index, RUN)
            run = d_slots[order[index, 0], order[index, 1]]
            d_t[:, cols] = run
            d[cols] = run.T
            delta[:, cols] = jnp.sum(run.astype(full) * dq_t[:, cols], axis=0, keepdims=True)
            return carry

        lax.fori_loop(0, runs, sort_run, 0)
        dq_t[...] = jnp.zeros_like(dq_t)

    scale = HEAD ** (-0.5)

    def key_tile(block):
        cut = tile_at(block, TILE)
        both = pl.ds(block * halves, halves)
        keys, values = k[both].reshape(TILE, HEAD), v[cut]
        keys_t = k_t[:, cut]
        dk[...] = jnp.zeros_like(dk)
        dv[...] = jnp.zeros_like(dv)

        def query_tile(index, diagonal):
            cols = tile_at(index, TILE)
            scores = dot_f32(keys, q_t[:, cols]) * (scale * LOG2_E)
            if diagonal:
                scores = causal(scores)
            probs = jnp.exp2(scores - lse[:, cols])
            dv[...] += dot_f32(probs.astype(low), d[cols])
            grad_probs = dot_f32(values, d_t[:, cols])
            grad_scores = (probs * (grad_probs - delta[:, cols])).astype(low)
            dk[...] += dot_f32(grad_scores, q[cols])
            dq_t[:, cols] += dot_f32(keys_t, grad_scores)

        query_tile(block, True)

        def later(index, inner):
            query_tile(index, False)
            return inner

        lax.fori_loop(block + 1, tiles, later, 0)
        for kind, value in enumerate(((dk[...] * scale).T.astype(low), dv[...].T.astype(low))):
            for half in range(halves):
                dkv_sorted[block * halves + half, kind] = value[:, half * RUN : (half + 1) * RUN]

    def key_tiles(start, stop):
        def one(block, carry):
            key_tile(block)
            return carry

        lax.fori_loop(start, stop, one, 0)

    swap = remote(dkv_slots.at[:, :, 1 - core], dkv_other, send_x, recv_x, sibling)
    dq_copies = return_copies(dq_slots, dq_own, send_q, recv_q)
    slot, owner = lax.rem(spot, 4), spot // 4
    dkv_copies = []
    for step in range(8):
        chip = lax.rem(spot + step, 8)
        parts = (
            dkv_slots.at[:, chip, core],
            dkv_own.at[slot, :, core],
            send_k.at[step],
            recv_k.at[slot, core],
            (row, chip, owner),
        )
        dkv_copies.append((parts, (owner == core) if step == 0 else False))

    def send_back():
        def unsort_run(run, carry):
            index = ids[run]
            for kind in range(2):
                dkv_slots[kind, run // per_device, run % per_device] = dkv_sorted[index, kind]
            return carry

        lax.fori_loop(0, runs, unsort_run, 0)
        swap.start()

        def turn_run(index, carry):
            value = dq_t[:, tile_at(index, RUN)] * scale
            d_slots[index // per_device, index % per_device] = value.astype(low)
            return carry

        lax.fori_loop(0, runs, turn_run, 0)

        def unsort_queries(run, carry):
            value = d_slots[order[runs + run, 0], order[runs + run, 1]]
            dq_slots[run // per_device, run % per_device] = value
            return carry

        lax.fori_loop(0, runs, unsort_queries, 0)
        start_return(dq_copies)

    def add_pairs():
        swap.wait()
        for chip in range(8):
            both = dkv_slots[:, chip, core].astype(full) + dkv_other[:, chip].astype(full)
            dkv_slots[:, chip, core] = both.astype(low)
        start_return(dkv_copies)


    def feed_forward():
        row_products(2 * FEED, 2, 1)
        for group in range(4):
            load_group(group).start()

    save_layer = pltpu.make_async_copy(part, layer_out, save_sem)

    def finish_layer():
        for index in range(4):
            pair_copy(index, 1).wait()
        pieces = width // PIECE

        def load_piece(index):
            lanes = pl.ds(index * PIECE, PIECE)
            return pltpu.make_async_copy(
                middle.at[:, lanes], middle_ring.at[index % 2], load_ring.at[index % 2]
            )

        load_piece(0).start()
        for index in range(pieces):
            if index + 1 < pieces:
                load_piece(index + 1).start()
            load_piece(index).wait()
            cut = pl.ds(index * PIECE, PIECE)
            value = part[:, cut].astype(full) + part_other[1, :, cut].astype(full)
            part[:, cut] = (value + middle_ring[index % 2]).astype(low)
        save_layer.start()


    def load_group(group):
        lanes = pl.ds(group * 4 * HEAD, 4 * HEAD)
        return pltpu.make_async_copy(
            near.at[:, :, :, :, lanes], weight.at[group], load_w.at[group]
        )

    load_mixed = pltpu.make_async_copy(
        mixed_low, right.at[:, pl.ds(qkv_width, out_width)], loads.at[0]
    )

    def project_back():
        load_mixed.start()
        for head in range(8):
            remote(
                dq_own.at[head], dq_own.at[head], send_q.at[0], recv_q.at[head], sibling
            ).wait_recv()
        for slot_in in range(4):
            for core_in in range(2):
                target = dkv_own.at[slot_in, :, core_in]
                remote(
                    target, target, send_k.at[0], recv_k.at[slot_in, core_in], sibling
                ).wait_recv()
        for group in range(4):
            for run in range(per_device):
                cols = slice(run * RUN, (run + 1) * RUN)
                turned = []
                for head in range(4):
                    if group < 2:
                        value = dq_own[4 * group + head, run]
                    else:
                        value = dkv_own[head, group - 2, run]
                    if group < 3:
                        front, back = value[:HALF].astype(full), value[HALF:].astype(full)
                        cos_part, sin_part = tables[0, :, cols], tables[1, :, cols]
                        turned.append((front * cos_part + back * sin_part).astype(low))
                        turned.append((back * cos_part - front * sin_part).astype(low))
                    else:
                        turned.append(value)
                right[cols, group * 4 * HEAD : (group + 1) * 4 * HEAD] = jnp.concatenate(
                    turned, axis=0
                ).T
        load_mixed.wait()

    def project_normed():
        save_layer.wait()
        for group in range(4):
            load_group(group).wait()
        stage(tokens).start()

        def block(index, carry):
            term = jnp.zeros((rows, quarter), full)
            for group in range(4):
                held = weight[group, index // 2, pl.ds(2 * lax.rem(index, 2), 2)]
                term = term + contract_cols(
                    right[:, group * 4 * HEAD : (group + 1) * 4 * HEAD],
                    held.reshape(quarter, 4 * HEAD),
                )
            part[:, tile_at(index, quarter)] = term.astype(low)
            pair_copy(index, 0).start()
            return carry

        lax.fori_loop(0, 4, block, 0)

    def save_input(index):
        cut = tile_at(index, rows // 8)
        slot = lax.rem(index, 2)
        return pltpu.make_async_copy(
            input_ring.at[slot], input_grad.at[cut], save_rows.at[slot]
        )

    def norm_back():
        stage(tokens).wait()
        for index in range(4):
            pair_copy(index, 0).wait()
        chunk = rows // 8

        def block(index, gain_grad):
            cut = tile_at(index, chunk)
            grad = part[cut].astype(full) + part_other[0, cut].astype(full)
            values = staged[cut].astype(full)
            inverse = lax.rsqrt(jnp.mean(values * values, axis=-1, keepdims=True) + epsilon)
            unit = values * inverse
            scaled = grad * gains_in[0:1]
            mean = jnp.mean(scaled * unit, axis=-1, keepdims=True)
            result = total[cut] + inverse * (scaled - unit * mean)

            @pl.when(index >= 2)
            def _():
                save_input(index - 2).wait()

            input_ring[lax.rem(index, 2)] = result.reshape(chunk, 1, width)
            save_input(index).start()
            return gain_grad + jnp.sum(grad * unit, axis=0, keepdims=True)

        gain_one_grad = lax.fori_loop(0, 8, block, jnp.zeros((1, width), full))
        lines = jnp.concatenate(
            [gain_one_grad, gain_two_grad[...], jnp.zeros((6, width), full)], axis=0
        )
        gain_columns[...] = lines.T
        for shard in range(16):
            held = gain_columns[shard * share : (shard + 1) * share]
            gain_messages[shard] = jnp.pad(held, ((0, WIDE - share), (0, 0))).T
        for copy in gain_copies:
            copy.start()
        gain_all[own_shard()] = gain_messages[own_shard()]

    gain_copies, gain_from = exchange_messages(
        lambda shard: gain_messages.at[shard], gain_all, send_gain, recv_gain
    )

    def finish_gains():
        for wait in gain_from:
            wait()
        gain_out[...] = jnp.sum(gain_all[...], axis=0)

    def take_normed():
        stage(normed_in).start()
        stage(normed_in).wait()
        turn_left(left_t, 2, staged)

    def start_forward():
        for piece in range(4):
            load_blocks(0, piece, 2 * FEED, 2)

    for copy in first_loads:
        copy.start()
    stage(cotangent).start()
    for piece in range(4):
        load_blocks(0, piece, 0, 4)
    for copy in early_loads:
        copy.start()
    greet(group_others())
    first_loads[0].wait()
    first_loads[1].wait()

    def wait_right():
        for copy in first_loads[2:]:
            copy.wait()

    plan = {
        2: [wait_right, second_back],
        3: [middle_back],
        4: [prepare],
        5: [start_forward, take_cotangents],
    }
    tiles_from, tile_ranges = 5, ((0, 1), (1, 2), (2, 3), (3, 5), (5, 8))
    later = {
        9: [send_back],
        11: [add_pairs, feed_forward, finish_layer, take_normed],
        12: [project_back],
        15: [lambda: turn_left(left_t, 0, grad_mid), project_normed],
        16: [norm_back],
        n + LAST - 1: [finish_gains],
    }

    def run(step, carry):
        for when, tasks in plan.items():

            @pl.when(step == when)
            def _():
                for task in tasks:
                    task()

        @pl.when(jnp.logical_and(step >= tiles_from, step < tiles_from + len(tile_ranges)))
        def _():
            start, stop = 0, 0
            for index, (first_tile, past_tile) in enumerate(tile_ranges):
                start = jnp.where(step == tiles_from + index, first_tile, start)
                stop = jnp.where(step == tiles_from + index, past_tile, stop)
            key_tiles(start, stop)

        for when, tasks in later.items():

            @pl.when(step == when)
            def _():
                for task in tasks:
                    task()

        sums.turn(step)
        return carry

    lax.fori_loop(0, n + LAST, run, 0)
    for index in (6, 7):
        save_input(index).wait()
    for copy in gain_copies:
        copy.wait_send()
    for step in (n - 2, n - 1):
        sums.each_save(step, lambda copy: copy.wait())
    for copies in (d_copies, dq_copies, dkv_copies):
        for parts, is_self in copies:
            if is_self is False:
                remote(*parts).wait_send()
            else:

                @pl.when(jnp.logical_not(is_self))
                def _():
                    remote(*parts).wait_send()


def backward(order, ids, *arrays):
    dma = pltpu.SemaphoreType.DMA
    vmem = pltpu.VMEM
    low, full = jnp.bfloat16, jnp.float32
    q_sorted, k_sorted, v_sorted, mixed_t, lse, cotangent, left, normed, right = arrays[:9]
    mixed_low, middle, near, far, tokens, gains, tables = arrays[9:]
    rows, width = cotangent.shape
    length = 8 * rows
    share = width // 16
    feed, query, out_width = right.shape[1] // 3, 8 * HEAD, mixed_low.shape[1]
    quarter = 4 * share
    per_device = rows // RUN
    heads = (8, per_device, HEAD, RUN)
    tall, flat = (length, HEAD), (HEAD, length)
    by_run = (length // RUN, RUN, HEAD)
    block = (rows, width)
    smem_spec = pl.BlockSpec(memory_space=pltpu.SMEM)
    shape = jax.ShapeDtypeStruct
    return pl.pallas_call(
        backward_kernel,
        in_specs=[smem_spec] * 2 + [any_spec()] * 14 + [vmem_spec()] * 2,
        out_specs=[any_spec()] * 9 + [vmem_spec()],
        out_shape=[
            shape((rows, 1, width), full),
            shape(block, low),
            *[
                shape((share, wide), full)
                for wide in (feed, feed, feed, query, query // 2, query // 2, out_width)
            ],
            shape((8, WIDE), full),
        ],
        scratch_shapes=[
            vmem(tall, low),
            vmem(flat, low),
            vmem(by_run, low),
            vmem(flat, low),
            vmem(tall, low),
            vmem(heads, low),
            vmem(heads, low),
            vmem(tall, low),
            vmem(flat, low),
            vmem(flat, full),
            vmem((1, length), full),
            vmem((1, length), full),
            vmem((TILE, HEAD), full),
            vmem((TILE, HEAD), full),
            vmem(heads, low),
            vmem((length // RUN, 2, HEAD, RUN), low),
            vmem((2,) + heads, low),
            vmem((2, 8, HEAD, RUN), low),
            vmem(heads, low),
            vmem((4, 2, per_device, HEAD, RUN), low),
            vmem((4, 2, 4, 2, share, 4 * HEAD), low),
            vmem((2, rows, PIECE), full),
            vmem((2, rows // 8, 1, width), full),
            vmem(block, low),
            vmem((2,) + block, low),
            vmem(block, full),
            vmem(block, low),
            vmem(block, low),
            vmem((1, width), full),
            vmem((3, 2, 2, quarter, rows), low),
            vmem(right.shape, low),
            vmem((width, 8), full),
            vmem((16, 8, WIDE), full),
            vmem((16, 8, WIDE), full),
            vmem((2, share, 2 * PIECE), full),
            vmem((3, 2, 2, quarter, PIECE), low),
            vmem((6, 2, 2, quarter, PIECE), low),
            vmem((3, 2, quarter, PIECE), low),
            vmem((6, 2, quarter, PIECE), low),
            vmem((4, 2, quarter, PIECE), low),
            vmem((4, 2, 3, share, PIECE), low),
            dma((7,)),
            dma((5,)),
            dma((16,)),
            dma((16,)),
            dma(()),
            dma((4,)),
            dma((2,)),
            dma((2,)),
            dma(()),
            dma((4, 2)),
            dma((8,)),
            dma((8,)),
            dma((8,)),
            dma(()),
            dma(()),
            dma((8,)),
            dma((4, 2)),
            dma((4,)),
            dma((2, 4)),
            dma((2, 3)),
            dma((3, 2)),
            dma((6, 2)),
            dma((3, 2)),
            dma((6, 2)),
            dma((4, 2, 3)),
            dma((4, 2, 3)),
        ],
        compiler_params=pltpu.CompilerParams(
            collective_id=2, has_side_effects=True, vmem_limit_bytes=62 * 1024 * 1024
        ),
        name="backward",
    )(
        order,
        ids,
        *arrays,
    )


def deliver_kernel(count, *refs):
    arrays, gain_grads = refs[:count], refs[count]
    results, gain_one, gain_two = refs[count + 1 : 2 * count + 1], refs[2 * count + 1], refs[2 * count + 2]
    held, loads, saves = refs[2 * count + 3 : 3 * count + 3], refs[-2], refs[-1]
    into, out = [], []
    for index in range(count):
        rows = arrays[index].shape[0]
        pieces = rows // 128 if rows % 128 == 0 else 1
        for piece in range(pieces):
            cut = pl.ds(piece * (rows // pieces), rows // pieces)
            place = index, piece
            into.append(
                pltpu.make_async_copy(
                    arrays[index].at[cut], held[index].at[cut], loads.at[place]
                )
            )
            out.append(
                pltpu.make_async_copy(
                    held[index].at[cut], results[index].at[cut], saves.at[place]
                )
            )
    for copy in into:
        copy.start()
    share = gain_one.shape[1]
    gain_one[...] = gain_grads[0:1, :share]
    gain_two[...] = gain_grads[1:2, :share]
    for came, goes in zip(into, out):
        came.wait()
        goes.start()
    for goes in out:
        goes.wait()


def deliver(arrays, gain_grads, share):
    count = len(arrays)
    shape = jax.ShapeDtypeStruct
    dma = pltpu.SemaphoreType.DMA
    return pl.pallas_call(
        functools.partial(deliver_kernel, count),
        in_specs=[any_spec()] * count + [vmem_spec()],
        out_specs=[any_spec()] * count + [vmem_spec()] * 2,
        out_shape=[shape(array.shape, array.dtype) for array in arrays]
        + [shape((1, share), jnp.float32)] * 2,
        scratch_shapes=[pltpu.VMEM(array.shape, array.dtype) for array in arrays]
        + [dma((count, 4)), dma((count, 4))],
        compiler_params=pltpu.CompilerParams(vmem_limit_bytes=VMEM_LIMIT),
        name="deliver",
    )(*arrays, gain_grads)


def by_heads(
    tokens,
    positions,
    gain_one,
    gain_two,
    w_query,
    w_key,
    w_value,
    w_out,
    w_gate,
    w_up,
    w_down,
    cotangent,
):
    rows, _, width = tokens.shape
    share = gain_one.shape[0]
    flat_in = tokens.reshape(rows, width)
    (
        near,
        far,
        normed,
        q_sorted,
        k_sorted,
        v_sorted,
        mixed_t,
        lse,
        mixed_low,
        middle,
        second,
        right,
        gains,
        tables,
        left,
        order,
        ids,
    ) = forward(
        flat_in,
        positions.reshape(1, rows),
        gain_one.reshape(1, share),
        gain_two.reshape(1, share),
        w_query,
        w_key,
        w_value,
        w_out.T,
        w_gate,
        w_up,
        w_down.T,
        cotangent.reshape(rows, width),
    )
    input_grad, layer_out, *grads, gain_grads = backward(
        order,
        ids,
        q_sorted,
        k_sorted,
        v_sorted,
        mixed_t,
        lse,
        cotangent.reshape(rows, width),
        left,
        normed,
        right,
        mixed_low,
        middle,
        near,
        far,
        flat_in,
        gains,
        tables,
    )
    input_grad, layer_out, *grads, grad_one, grad_two = deliver(
        [input_grad, layer_out, *grads], gain_grads, share
    )
    grad_gate, grad_up, grad_down, grad_query, grad_key, grad_value, grad_out = grads
    return (
        layer_out.reshape(rows, 1, width),
        input_grad,
        grad_one.reshape(share),
        grad_two.reshape(share),
        grad_query,
        grad_key,
        grad_value,
        grad_out.T,
        grad_gate,
        grad_up,
        grad_down.T,
    )


def solution(mesh):
    sizes = (mesh.shape["dp"], mesh.shape["context"], mesh.shape["tensor"])
    return jax.shard_map(
        by_heads if sizes == (2, 8, 2) else on_device,
        mesh=mesh,
        in_specs=(
            P("context", "dp", None),
            P("context", "dp"),
            P(("dp", "context")),
            P(("dp", "context")),
            P(("dp", "context"), "tensor"),
            P(("dp", "context"), "tensor"),
            P(("dp", "context"), "tensor"),
            P("tensor", ("dp", "context")),
            P(("dp", "context"), "tensor"),
            P(("dp", "context"), "tensor"),
            P("tensor", ("dp", "context")),
            P("context", "dp", None),
        ),
        out_specs=(
            P("context", "dp", None),
            P("context", "dp", None),
            P(("dp", "context")),
            P(("dp", "context")),
            P(("dp", "context"), "tensor"),
            P(("dp", "context"), "tensor"),
            P(("dp", "context"), "tensor"),
            P("tensor", ("dp", "context")),
            P(("dp", "context"), "tensor"),
            P(("dp", "context"), "tensor"),
            P("tensor", ("dp", "context")),
        ),
        check_vma=False,
    )
```

profile of v0, /device:TPU:4, one launch (start us, length us, event | category | flops | bytes accessed | tf_op | source)
XLA Modules:
  0.0 507.3 jit_solution(13241741993953305231)
XLA Ops:
  0.6 240.8 %forward.1 = (bf16[2,4,2,96,2304]{4,3,2,1,0:T(8,128)(2,1)}, bf16[2,4,2,96,6144]{4,3,2,1,0:T(8,128)(2,1)}, bf16[512,1536]{1,0:T(8,128)(2,1)}, bf16[96,4096]{1,0:T...) custom-call(bf16[512,1536]{1,0:T(8,128)(2,1)} %bitcast.12, ...), custom_call_target="tpu_custom_call" | custom-call | tf_op jit(solution)/shard_map/forward/pallas_call | solution.py:1309
  241.5 257.9 %backward.1 = (f32[512,1,1536]{2,1,0:T(1,128)}, bf16[512,1536]{1,0:T(8,128)(2,1)}, f32[96,2048]{1,0:T(8,128)}, f32[96,2048]{1,0:T(8,128)}, f32[96,2048]{1,0:T(8,...) custom-call(s32[32,2]{1,0:T(8,128)} %get-tuple-element.48.order, ...), custom_call_target="tpu_custom_call" | custom-call | tf_op jit(solution)/shard_map/backward/pallas_call | solution.py:2226
  499.4 7.8 %deliver.1 = (f32[512,1,1536]{2,1,0:T(1,128)}, bf16[512,1536]{1,0:T(8,128)(2,1)}, f32[96,2048]{1,0:T(8,128)}, f32[96,2048]{1,0:T(8,128)}, f32[96,2048]{1,0:T(8,1...) custom-call(f32[512,1,1536]{2,1,0:T(1,128)} %get-tuple-element.64.re, ...), custom_call_target="tpu_custom_call" | custom-call | tf_op jit(solution)/shard_map/deliver/pallas_call | solution.py:2356
where the time goes:
time: 508 us; the launch traced here: 507 us
  Pallas kernels  506 us (100%)
    pallas_call x1, Pallas kernels, backward(): pl.pallas_call(backward_kernel, in_specs=[smem_spec] * 2 + [any_spec()] *...  258 us
    pallas_call x1, Pallas kernels, forward(): pl.pallas_call(forward_kernel, in_specs=[vmem_spec()] * 5 + [any_spec()]...  241 us

commit v1 on v0

--- a/solution.py
+++ b/solution.py
@@ -1515,7 +1515,7 @@
     def third_copy(self, step, kind, k):
         row, level, column, beside_x, beside_y, along_z = neighbours()
         target = lax.rem(level + k + 1, 4)
-        out, into = lax.rem(step, 4), lax.rem(step, 4)
+        out, into = lax.rem(step, 4), lax.rem(step, 5)
         return remote(
             self.kept.at[out, kind, pl.ds(pl.multiple_of(target * self.share, 16), self.share)],
             self.recv_three.at[into, kind, k],
@@ -1582,7 +1582,7 @@
 
     def last(self, step):
         level = neighbours()[1]
-        came, keep = lax.rem(step, 4), lax.rem(step, 4)
+        came, keep = lax.rem(step, 5), lax.rem(step, 4)
         mine = pl.ds(pl.multiple_of(level * self.share, 16), self.share)
 
         @pl.when(step >= 2)
@@ -1600,14 +1600,17 @@
         self.each_save(step, lambda copy: copy.start())
 
     def turn(self, step):
-        for stage, lag in (
-            (self.first, 0),
-            (self.second, SECOND),
-            (self.third, THIRD),
-            (self.last, LAST),
+        n, hurry = self.n, self.n - 1
+        for stage, lag, begin, end in (
+            (self.first, 0, 0, n),
+            (self.second, SECOND, SECOND, n + SECOND),
+            (self.third, THIRD, THIRD, hurry + 1),
+            (self.third, THIRD - 1, hurry, n + THIRD - 1),
+            (self.last, LAST, LAST, hurry + 2),
+            (self.last, LAST - 1, hurry + 1, n + LAST - 1),
         ):
 
-            @pl.when(jnp.logical_and(step >= lag, step < self.n + lag))
+            @pl.when(jnp.logical_and(step >= begin, step < end))
             def _():
                 stage(step - lag)
 
@@ -2158,7 +2161,7 @@
         12: [project_back],
         15: [lambda: turn_left(left_t, 0, grad_mid), project_normed],
         16: [norm_back],
-        n + LAST - 1: [finish_gains],
+        n + LAST - 2: [finish_gains],
     }
 
     def run(step, carry):
@@ -2187,7 +2190,7 @@
         sums.turn(step)
         return carry
 
-    lax.fori_loop(0, n + LAST, run, 0)
+    lax.fori_loop(0, n + LAST - 1, run, 0)
     for index in (6, 7):
         save_input(index).wait()
     for copy in gain_copies:
@@ -2277,7 +2280,7 @@
             vmem((3, 2, quarter, PIECE), low),
             vmem((6, 2, quarter, PIECE), low),
             vmem((4, 2, quarter, PIECE), low),
-            vmem((4, 2, 3, share, PIECE), low),
+            vmem((5, 2, 3, share, PIECE), low),
             dma((7,)),
             dma((5,)),
             dma((16,)),
@@ -2303,7 +2306,7 @@
             dma((3, 2)),
             dma((6, 2)),
             dma((4, 2, 3)),
-            dma((4, 2, 3)),
+            dma((5, 2, 3)),
         ],
         compiler_params=pltpu.CompilerParams(
             collective_id=2, has_side_effects=True, vmem_limit_bytes=62 * 1024 * 1024

time: 508 us -> 503 us (level)
  no operation moved by 1% of the time
where the time goes in v1:
time: 503 us
  Pallas kernels  502 us (100%)
    pallas_call x1, Pallas kernels, backward(): pl.pallas_call(backward_kernel, in_specs=[smem_spec] * 2 + [any_spec()] *...  253 us
    pallas_call x1, Pallas kernels, forward(): pl.pallas_call(forward_kernel, in_specs=[vmem_spec()] * 5 + [any_spec()]...  241 us

profile of v1, /device:TPU:4, one launch (start us, length us, event | category | flops | bytes accessed | tf_op | source)
XLA Modules:
  0.0 502.5 jit_solution(8944526361452647681)
XLA Ops:
  0.6 240.8 %forward.1 = (bf16[2,4,2,96,2304]{4,3,2,1,0:T(8,128)(2,1)}, bf16[2,4,2,96,6144]{4,3,2,1,0:T(8,128)(2,1)}, bf16[512,1536]{1,0:T(8,128)(2,1)}, bf16[96,4096]{1,0:T...) custom-call(bf16[512,1536]{1,0:T(8,128)(2,1)} %bitcast.12, ...), custom_call_target="tpu_custom_call" | custom-call | tf_op jit(solution)/shard_map/forward/pallas_call | solution.py:1309
  241.5 253.1 %backward.1 = (f32[512,1,1536]{2,1,0:T(1,128)}, bf16[512,1536]{1,0:T(8,128)(2,1)}, f32[96,2048]{1,0:T(8,128)}, f32[96,2048]{1,0:T(8,128)}, f32[96,2048]{1,0:T(8,...) custom-call(s32[32,2]{1,0:T(8,128)} %get-tuple-element.48.order, ...), custom_call_target="tpu_custom_call" | custom-call | tf_op jit(solution)/shard_map/backward/pallas_call | solution.py:2229
  494.6 7.8 %deliver.1 = (f32[512,1,1536]{2,1,0:T(1,128)}, bf16[512,1536]{1,0:T(8,128)(2,1)}, f32[96,2048]{1,0:T(8,128)}, f32[96,2048]{1,0:T(8,128)}, f32[96,2048]{1,0:T(8,1...) custom-call(f32[512,1,1536]{2,1,0:T(1,128)} %get-tuple-element.64.re, ...), custom_call_target="tpu_custom_call" | custom-call | tf_op jit(solution)/shard_map/deliver/pallas_call | solution.py:2359
